TPU v7x, 256 devices: a whole 4x4x8 slice. The times are simulated.
256 devices in a mesh: row: 8 (over z), col: 16 (over y, x), layer: 2 (over core).
Axes of the slice: x: 4, y: 4, z: 8, core: 2. Of those that a mesh axis runs over, the one named last changes fastest.
Arguments:
- density: bfloat16 [8192, 8192], P('row', ('col', 'layer')), may hold values from -3 to 3
- block_mask: int32 [64, 64], P('row', ('col', 'layer')), may hold values from 0 to 1, as said below
- keep_mask: int32 [64, 64], P('row', ('col', 'layer')), may hold values 0 or 1
- branch_flag: int32 [64], P('row'), may hold values from 0 to 1
Outputs:
- updated: float32 [8192, 8192], P('row', ('col', 'layer'))
- trace_new: float32 [], replicated
Inputs may be any that keep to these rules, and one draw needn't show every extreme that they name: `block_mask`: symmetric, 1 on the diagonal; 1 where two blocks' centres in a periodic box lie within a cutoff distance of each other, else 0; block labels are in no spatial order. `keep_mask`: 0 or 1 for each block.
All inputs are finite; a program needn't handle non-finite values.
Results may differ from a plain program's by a relative error of at most 0.0004.
Values may be sent and summed in bfloat16 or wider, within the bound.
No kernel may reach another device: no remote copies, remote signals or barrier semaphores. Data moves between devices by JAX's collectives and lax.ppermute only.
A program may use at most 64 MiB of HBM per device.

v0:
```python
import functools
import jax
import jax.numpy as jnp
from jax import lax
from jax.sharding import Mesh
from jax.sharding import PartitionSpec as P

BLK = 128
COL = ("col_0", "col_1")
ROW_COL_LAYER = ("row", "col_0", "col_1", "layer")
COL_LAYER = ("col_0", "col_1", "layer")


def partner(value, axis, stride):
    mask = 2**stride
    pairs = [(source, source ^ mask) for source in range(lax.axis_size(axis))]
    return lax.ppermute(value, axis, pairs)


def split_up(value, dim, devices):
    shape = value.shape
    pieces = value.reshape(*shape[:dim], devices, shape[dim] // devices, *shape[dim + 1 :])
    return jnp.moveaxis(pieces, dim, 0)


def sum_at_owner(value, axis, dim):
    devices = lax.axis_size(axis)
    pieces = lax.all_to_all(split_up(value, dim, devices), axis, 0, 0, tiled=True)
    return jnp.sum(pieces, axis=0)


def over_axes(value, axes):
    return functools.reduce(lax.psum, axes, value)


def expand_mask(block_mask):
    return jnp.repeat(jnp.repeat(block_mask, BLK, axis=0), BLK, axis=1)


def on_device(density, block_mask, keep_mask, branch_flag):
    row_count = density.shape[0]
    col_width = density.shape[1]
    masked = density * expand_mask(block_mask).astype(jnp.bfloat16)
    col_panel = lax.all_gather(masked, "row", axis=0, tiled=True)
    layer_index = lax.axis_index("layer")
    col_groups = lax.axis_size(COL)
    grouped = col_panel.reshape(col_groups, 2, col_width, col_width)
    own_rows = lax.dynamic_index_in_dim(grouped, layer_index, 1, keepdims=False)
    outgoing = lax.dynamic_index_in_dim(grouped, 1 - layer_index, 1, keepdims=False)
    peer_rows = partner(outgoing, "layer", 0)
    own_rows = own_rows.reshape(col_groups * col_width, col_width)
    peer_rows = peer_rows.reshape(col_groups * col_width, col_width)
    lead_part = jnp.where(layer_index == 0, own_rows, peer_rows)
    tail_part = jnp.where(layer_index == 0, peer_rows, own_rows)
    inner_panel = jnp.concatenate([lead_part, tail_part], axis=1)
    partial_value = jnp.dot(
        lax.all_gather(masked, COL, axis=1, tiled=True),
        inner_panel,
        preferred_element_type=jnp.float32,
    )
    product = sum_at_owner(partial_value, "layer", 1)
    doubled = 2.0 * masked.astype(jnp.float32) - product
    flag_rows = jnp.repeat(branch_flag, BLK)[:, None]
    chosen = jnp.where(flag_rows == 1, product, doubled)
    updated = chosen * expand_mask(keep_mask).astype(jnp.float32)
    row_anchor = lax.axis_index("row") * row_count
    col_anchor = (
        lax.axis_index(COL) * lax.axis_size("layer") + lax.axis_index("layer")
    ) * col_width
    row_ids = row_anchor + jnp.arange(row_count, dtype=jnp.int32)[:, None]
    col_ids = col_anchor + jnp.arange(col_width, dtype=jnp.int32)[None, :]
    local_trace = jnp.sum(jnp.where(row_ids == col_ids, updated, 0.0))
    trace_new = over_axes(local_trace, ROW_COL_LAYER)
    return (updated, trace_new)


def solution(mesh):
    split = Mesh(
        mesh.devices.reshape(mesh.shape["row"], 4, 4, mesh.shape["layer"]),
        ("row", "col_0", "col_1", "layer"),
    )
    in_specs = (P("row", COL_LAYER), P("row", COL_LAYER), P("row", COL_LAYER), P("row"))
    out_specs = (P("row", COL_LAYER), P())
    return jax.shard_map(
        on_device, mesh=split, in_specs=in_specs, out_specs=out_specs, check_vma=False
    )
```

profile of v0, /device:TPU:1, one launch (start us, length us, event | category | flops | bytes accessed | tf_op | source)
XLA Modules:
  0.0 212.9 jit_solution(15898853218652076611)
XLA Ops:
  7.2 1.2 copy.10
  8.5 0.7 convert_element_type.25
  9.1 0.1 broadcast_bitcast_fusion.1
  9.2 0.8 bitcast_multiply_fusion
  10.1 0.7 all-gather.3.cloned.1.call-update
  10.9 58.0 %all-gather.5.cloned.1.call-done = bf16[8192,256]{0,1:T(8,128)(2,1)} async-done(((bf16[1024,256]{0,1:T(8,128)(2,1)}), bf16[8192,256]{0,1:T(8,128)(2,1)}) %all-gather.5.cloned.1.call-update) | async-done | bytes 4194320 | tf_op jit(solution)/shard_map/all_gather | solution.py:44
  68.9 7.8 %reshape.44 = bf16[16,2,256,256]{2,1,0,3:T(2,128)(2,1)} reshape(bf16[8192,256]{0,1:T(8,128)(2,1)} %all-gather.5.cloned.1.call-done) | data formatting | bytes 8388608 | tf_op jit(solution)/shard_map/reshape | solution.py:47
  76.7 13.4 %constant_dynamic-slice_fusion.1 = (bf16[16,1,256,256]{2,1,0,3:T(2,128)(2,1)}, bf16[16,1,256,256]{2,1,0,3:T(2,128)(2,1)}) fusion(bf16[16,2,256,256]{2,1,0,3:T(2,128)(2,1)} %reshape.44, s32[]{:T(128)S(6)} %select_n.28, s32[]{:T(128)S(6)} %select_n.29), kind=kLoop, calls=%fused_computation.18 | loop fusion | bytes 8388616 | tf_op jit(solution)/shard_map/jit(dynamic_index_in_dim)/dynamic_slice | solution.py:48
  90.1 10.5 %copy.15 = bf16[16,1,256,256]{3,2,0,1:T(8,128)(2,1)} copy(bf16[16,1,256,256]{2,1,0,3:T(2,128)(2,1)} %get-tuple-element.11) | data formatting | bytes 4194304
  100.6 0.7 collective-permute-start
  101.3 0.1 broadcast_bitcast_fusion
  101.4 0.1 broadcast_bitcast_fusion.2
  101.5 9.0 %copy.14 = bf16[16,1,256,256]{3,2,0,1:T(8,128)(2,1)S(1)} copy(bf16[16,1,256,256]{2,1,0,3:T(2,128)(2,1)} %get-tuple-element.10) | data formatting | bytes 4194304
  110.5 3.8 %bitcast_select_fusion.1 = (bf16[4096,256]{1,0:T(8,128)(2,1)}, bf16[4096,256]{1,0:T(8,128)(2,1)}) fusion(bf16[16,256,256]{2,1,0:T(8,128)(2,1)} %collective-permute-done, bf16[16,1,256,256]{3,2,0,1:T(8,128)(2,1)S(1)} %copy.14, pred[]{:T(512)S(6)} %eq.35), kind=kLoop, calls=%fused_computation.5 | loop fusion | flops 2097152 | bytes 8388609 | tf_op jit(solution)/shard_map/jit(_where)/select_n | solution.py:53
  114.3 31.4 %all-gather.3.cloned.1.call-done = bf16[1024,4096]{0,1:T(8,128)(2,1)} async-done(((bf16[1024,256]{0,1:T(8,128)(2,1)}), bf16[1024,4096]{0,1:T(8,128)(2,1)}) %all-gather.3.cloned.1.call-update) | async-done | bytes 8388624 | tf_op jit(solution)/shard_map/all_gather | solution.py:57
  145.7 8.3 %fusion = f32[1024,512]{0,1:T(8,128)S(1)} fusion(bf16[1024,4096]{0,1:T(8,128)(2,1)} %all-gather.3.cloned.1.call-done, bf16[4096,256]{1,0:T(8,128)(2,1)} %get-tuple-element.9, bf16[4096,256]{1,0:T(8,128)(2,1)} %get-tuple-element.8), kind=kOutput, calls=%fused_computation | convolution fusion | flops 4303355904 | bytes 14680064 | tf_op jit(solution)/shard_map/dot_general | solution.py:56
  154.0 5.8 %all_to_all.5 = f32[2,1024,256]{1,2,0:T(8,128)S(1)} all-to-all(f32[2,1024,256]{1,2,0:T(8,128)S(1)} %bitcast.34), channel_id=1, replica_groups=mesh['row'=8,'col_0'=4,'col_1'=4,'layer'=2] {'layer'}, dimensions={0} | all-to-all | bytes 4194304 | tf_op jit(solution)/shard_map/all_to_all | solution.py:28
  159.8 1.2 reduce_sum.18
  161.0 2.3 %select_reduce_fusion = (f32[]{:T(128)}, f32[1024,256]{0,1:T(8,128)S(1)}) fusion(s32[1024]{0:T(1024)S(1)} %iota_add_fusion, s32[256]{0:T(256)S(1)} %iota_add_fusion.1, f32[1024,2]{0,1:T(2,128)S(1)} %bitcast.35, f32[1024,256]{0,1:T(8,128)} %reduce_sum.18, bf16[1024,256]{0,1:T(8,128)(2,1)S(1)} %copy-done, pred[1024]{0:T(1024)(128)(4,1)S(1)} %broadcast_bitcast_fusion.2), kind=kLoop, calls=%fused_computation.8 | loop fusion | flops 2097151 | bytes 2635780 | tf_op jit(solution)/shard_map/reduce_sum | solution.py:72
  163.3 14.6 %psum.28 = f32[]{:T(128)} all-reduce(f32[]{:T(128)} %get-tuple-element.6), channel_id=1, replica_groups=mesh['row'=8,'col_0'=4,'col_1'=4,'layer'=2] {'row'}, use_global_device_ids=true, to_apply=%region_2.3 | all-reduce | flops 1 | bytes 8 | tf_op jit(solution)/shard_map/psum | solution.py:33
  178.0 9.0 %psum.29 = f32[]{:T(128)} all-reduce(f32[]{:T(128)} %psum.28), channel_id=1, replica_groups=mesh['row'=8,'col_0'=4,'col_1'=4,'layer'=2] {'col_0'}, use_global_device_ids=true, to_apply=%region_3.4 | all-reduce | flops 1 | bytes 8 | tf_op jit(solution)/shard_map/psum | solution.py:33
  187.0 7.2 %psum.30 = f32[]{:T(128)} all-reduce(f32[]{:T(128)} %psum.29), channel_id=1, replica_groups=mesh['row'=8,'col_0'=4,'col_1'=4,'layer'=2] {'col_1'}, use_global_device_ids=true, to_apply=%region_4.5 | all-reduce | flops 1 | bytes 8 | tf_op jit(solution)/shard_map/psum | solution.py:33
  194.2 1.3 copy.13
  195.5 10.6 %psum.31 = f32[]{:T(128)} all-reduce(f32[]{:T(128)} %psum.30), channel_id=1, replica_groups=mesh['row'=8,'col_0'=4,'col_1'=4,'layer'=2] {'layer'}, use_global_device_ids=true, to_apply=%region_5.6 | all-reduce | flops 1 | bytes 8 | tf_op jit(solution)/shard_map/psum | solution.py:33
  (16 shorter events, 0.1 us)
Async XLA Ops:
  7.2 61.7 %all-gather.5.cloned.1.call-start = ((), (), s32[]{:S(2)}) async-start(), calls=%async_computation.2 | async-start | bytes 4718592 | tf_op jit(solution)/shard_map/all_gather | solution.py:44
  10.1 135.6 %all-gather.3.cloned.1.call-start = ((), (), s32[]{:S(2)}) async-start(), calls=%async_computation.1 | async-start | bytes 8912896 | tf_op jit(solution)/shard_map/all_gather | solution.py:57
  90.1 11.2 %copy-start.1 = (s32[8,2]{0,1:T(2,128)S(1)}, s32[8,2]{0,1:T(2,128)}, u32[]{:S(2)}) copy-start(s32[8,2]{0,1:T(2,128)} %param.6) | copy-start | bytes 196
  90.1 11.3 %copy-start.2 = (s32[8]{0:T(128)S(1)}, s32[8]{0:T(128)}, u32[]{:S(2)}) copy-start(s32[8]{0:T(128)} %param.7) | copy-start | bytes 100
  100.6 9.8 %collective-permute-start = (bf16[16,256,256]{2,1,0:T(8,128)(2,1)}, bf16[16,256,256]{2,1,0:T(8,128)(2,1)}, u32[]{:S(2)}, u32[]{:S(2)}) collective-permute-start(bf16[16,256,256]{2,1,0:T(8,128)(2,1)} %bitcast.3), channel_id=1, source_target_pairs={{0,1},{1,0},{2,3},{3,2},{4,5},{5,4},{6,7},{7,6},{8,9},{9,8},{10,11... | collective-permute-start | bytes 6291464 | tf_op jit(solution)/shard_map/ppermute | solution.py:17
  154.0 7.1 %copy-start = (bf16[1024,256]{0,1:T(8,128)(2,1)S(1)}, bf16[1024,256]{0,1:T(8,128)(2,1)}, u32[]{:S(2)}) copy-start(bf16[1024,256]{0,1:T(8,128)(2,1)} %bitcast_multiply_fusion) | copy-start | bytes 1572868
Sparse Core Ops, SparseCore 0:
  10.2 58.6 all-gather.4
  71.3 74.3 all-gather.2
where the time goes:
time: 214 us; the launch traced here: 213 us
  waiting for transfers between devices  90.1 us (42%)
  blocking collectives  47.2 us (22%)
  local copies, waits for them, and re-layouts  43.5 us (20%)
  between operations  14.1 us (7%)
  other arithmetic  8.9 us (4%)
  matrix products  8.26 us (4%)
    all_gather x1, waiting for transfers between devices, on_device(): col_panel = lax.all_gather(masked, 'row', axis=0, tiled=True)  58 us
    psum x4, blocking collectives, over_axes(): return functools.reduce(lax.psum, axes, value)  41.4 us
    all_gather x1, waiting for transfers between devices, on_device(): lax.all_gather(masked, COL, axis=1, tiled=True)  31.4 us
    unnamed x14, local copies, waits for them, and re-layouts  22.2 us
    dynamic_slice x1, local copies, waits for them, and re-layouts, on_device(): own_rows = lax.dynamic_index_in_dim(grouped, layer_index, 1, keepdims=False)  13.4 us
    dot_general x1, matrix products, on_device(): jnp.dot(lax.all_gather(masked, COL, axis=1, tiled=True), inner_panel, pre...  8.26 us
    reshape x1, local copies, waits for them, and re-layouts, on_device(): grouped = col_panel.reshape(col_groups, 2, col_width, col_width)  7.82 us
    all_to_all x1, blocking collectives, sum_at_owner(): lax.all_to_all(split_up(value, dim, devices), axis, 0, 0, tiled=True)  5.85 us
  transfers between devices with their start and end apart: 3, of which 2 were waited for; matrix products, arithmetic and copies ran while one was open for 21% of the time, Pallas kernels for 0%

commit v1 on v0

--- a/solution.py
+++ b/solution.py
@@ -41,7 +41,12 @@
     row_count = density.shape[0]
     col_width = density.shape[1]
     masked = density * expand_mask(block_mask).astype(jnp.bfloat16)
-    col_panel = lax.all_gather(masked, "row", axis=0, tiled=True)
+    ring = [masked]
+    for hop in range(7):
+        ring.append(lax.ppermute(ring[-1], "row", [(dev, (dev + 1) % 8) for dev in range(8)]))
+    col_panel = jnp.roll(
+        jnp.concatenate(ring[::-1], axis=0), (lax.axis_index("row") + 1) * ring[0].shape[0], axis=0
+    )
     layer_index = lax.axis_index("layer")
     col_groups = lax.axis_size(COL)
     grouped = col_panel.reshape(col_groups, 2, col_width, col_width)

time: 214 us -> 197 us (0.921)
  local copies, waits for them, and re-layouts: 43.5 us -> 21.1 us
  starting transfers between devices: 0.75 us -> 9.13 us
    ppermute x0 -> x7, waiting for transfers between devices: none -> 85.4 us  [on_device(): lax.ppermute(ring[-1], 'row', [(dev, (dev + 1) % 8) for dev in range(8)])]
    all_gather x1 -> x0, waiting for transfers between devices: 58 us -> none  [on_device(): col_panel = lax.all_gather(masked, 'row', axis=0, tiled=True)]
    all_gather x1, waiting for transfers between devices: 31.4 us -> 0.01 us  [on_device(): lax.all_gather(masked, COL, axis=1, tiled=True)]
    unnamed x14 -> x27, local copies, waits for them, and re-layouts: 22.2 us -> 8.48 us
    dynamic_slice x1, local copies, waits for them, and re-layouts: 13.4 us -> 3.95 us  [on_device(): own_rows = lax.dynamic_index_in_dim(grouped, layer_index, 1, keepdims=False)]
    dynamic_slice x0 -> x2, local copies, waits for them, and re-layouts: none -> 8.61 us  [on_device(): jnp.roll(jnp.concatenate(ring[::-1], axis=0), (lax.axis_index('row') + 1)...]
    reshape x1 -> x0, local copies, waits for them, and re-layouts: 7.82 us -> none  [on_device(): grouped = col_panel.reshape(col_groups, 2, col_width, col_width)]
    ppermute x1, starting transfers between devices: 0.67 us -> 6.54 us  [partner(): return lax.ppermute(value, axis, pairs)]
  transfers between devices with their start and end apart: 3 -> 9, of which waited for: 2 -> 8; matrix products, arithmetic and copies ran while one was open for 21% -> 11% of each run, Pallas kernels for 0% -> 0%
where the time goes in v1:
time: 197 us
  waiting for transfers between devices  89.4 us (45%)
  blocking collectives  45.5 us (23%)
  local copies, waits for them, and re-layouts  21.1 us (11%)
  between operations  14.2 us (7%)
  starting transfers between devices  9.13 us (5%)
  other arithmetic  9 us (5%)
  matrix products  8.26 us (4%)
    ppermute x7, waiting for transfers between devices, on_device(): lax.ppermute(ring[-1], 'row', [(dev, (dev + 1) % 8) for dev in range(8)])  85.4 us
    psum x4, blocking collectives, over_axes(): return functools.reduce(lax.psum, axes, value)  40.1 us
    dynamic_slice x2, local copies, waits for them, and re-layouts, on_device(): jnp.roll(jnp.concatenate(ring[::-1], axis=0), (lax.axis_index('row') + 1)...  8.61 us
    unnamed x27, local copies, waits for them, and re-layouts  8.48 us
    dot_general x1, matrix products, on_device(): jnp.dot(lax.all_gather(masked, COL, axis=1, tiled=True), inner_panel, pre...  8.26 us
    ppermute x1, starting transfers between devices, partner(): return lax.ppermute(value, axis, pairs)  6.54 us
    all_to_all x1, blocking collectives, sum_at_owner(): lax.all_to_all(split_up(value, dim, devices), axis, 0, 0, tiled=True)  5.42 us
    dynamic_slice x1, local copies, waits for them, and re-layouts, on_device(): own_rows = lax.dynamic_index_in_dim(grouped, layer_index, 1, keepdims=False)  3.95 us
  transfers between devices with their start and end apart: 9, of which 8 were waited for; matrix products, arithmetic and copies ran while one was open for 11% of the time, Pallas kernels for 0%

profile of v1, /device:TPU:1, one launch (start us, length us, event | category | flops | bytes accessed | tf_op | source)
XLA Modules:
  0.0 196.7 jit_solution(3059400100246512557)
XLA Ops:
  7.2 1.2 copy.12
  10.1 2.5 %collective-permute-start = (bf16[1024,256]{0,1:T(8,128)(2,1)}, bf16[1024,256]{0,1:T(8,128)(2,1)S(1)}, u32[]{:S(2)}, u32[]{:S(2)}) collective-permute-start(bf16[1024,256]{0,1:T(8,128)(2,1)} %bitcast_multiply_fusion), channel_id=1, source_target_pairs={{0,32},{32,64},{64,96},{96,128},{128,160},{160,192},{192,224},{224... | collective-permute-start | bytes 1572872 | tf_op jit(solution)/shard_map/ppermute | solution.py:46
  12.6 15.8 %collective-permute-done = bf16[1024,256]{0,1:T(8,128)(2,1)S(1)} collective-permute-done((bf16[1024,256]{0,1:T(8,128)(2,1)}, bf16[1024,256]{0,1:T(8,128)(2,1)S(1)}, u32[]{:S(2)}, u32[]{:S(2)}) %collective-permute-start) | collective-permute-done | bytes 524320 | tf_op jit(solution)/shard_map/ppermute | solution.py:46
  28.4 13.5 %collective-permute-done.1 = bf16[1024,256]{0,1:T(8,128)(2,1)S(1)} collective-permute-done((bf16[1024,256]{0,1:T(8,128)(2,1)S(1)}, bf16[1024,256]{0,1:T(8,128)(2,1)S(1)}, u32[]{:S(2)}, u32[]{:S(2)}) %collective-permute-start.1) | collective-permute-done | bytes 524320 | tf_op jit(solution)/shard_map/ppermute | solution.py:46
  41.9 12.6 %collective-permute-done.2 = bf16[1024,256]{0,1:T(8,128)(2,1)S(1)} collective-permute-done((bf16[1024,256]{0,1:T(8,128)(2,1)S(1)}, bf16[1024,256]{0,1:T(8,128)(2,1)S(1)}, u32[]{:S(2)}, u32[]{:S(2)}) %collective-permute-start.2) | collective-permute-done | bytes 524320 | tf_op jit(solution)/shard_map/ppermute | solution.py:46
  54.5 11.8 %collective-permute-done.3 = bf16[1024,256]{0,1:T(8,128)(2,1)S(1)} collective-permute-done((bf16[1024,256]{0,1:T(8,128)(2,1)S(1)}, bf16[1024,256]{0,1:T(8,128)(2,1)S(1)}, u32[]{:S(2)}, u32[]{:S(2)}) %collective-permute-start.3) | collective-permute-done | bytes 524320 | tf_op jit(solution)/shard_map/ppermute | solution.py:46
  66.3 10.9 %collective-permute-done.4 = bf16[1024,256]{0,1:T(8,128)(2,1)S(1)} collective-permute-done((bf16[1024,256]{0,1:T(8,128)(2,1)S(1)}, bf16[1024,256]{0,1:T(8,128)(2,1)S(1)}, u32[]{:S(2)}, u32[]{:S(2)}) %collective-permute-start.4) | collective-permute-done | bytes 524320 | tf_op jit(solution)/shard_map/ppermute | solution.py:46
  77.2 10.5 %collective-permute-done.5 = bf16[1024,256]{0,1:T(8,128)(2,1)} collective-permute-done((bf16[1024,256]{0,1:T(8,128)(2,1)S(1)}, bf16[1024,256]{0,1:T(8,128)(2,1)}, u32[]{:S(2)}, u32[]{:S(2)}) %collective-permute-start.5) | collective-permute-done | bytes 524320 | tf_op jit(solution)/shard_map/ppermute | solution.py:46
  87.7 10.4 %collective-permute-done.6 = bf16[1024,256]{0,1:T(8,128)(2,1)} collective-permute-done((bf16[1024,256]{0,1:T(8,128)(2,1)}, bf16[1024,256]{0,1:T(8,128)(2,1)}, u32[]{:S(2)}, u32[]{:S(2)}) %collective-permute-start.6) | collective-permute-done | bytes 524320 | tf_op jit(solution)/shard_map/ppermute | solution.py:46
  104.0 2.2 %constant_dynamic-slice_fusion.1 = bf16[8192,256]{0,1:T(8,128)(2,1)} fusion(bf16[16384,256]{0,1:T(8,128)(2,1)S(1)} %constant_dynamic-update-slice_fusion, s32[]{:T(128)S(6)} %select_n.42), kind=kLoop, calls=%fused_computation.35 | loop fusion | bytes 8388612 | tf_op jit(solution)/shard_map/jit(_roll_dynamic)/dynamic_slice | solution.py:47
  106.2 6.4 %copy.13 = bf16[8192,256]{1,0:T(8,128)(2,1)} copy(bf16[8192,256]{0,1:T(8,128)(2,1)} %constant_dynamic-slice_fusion.1) | data formatting | bytes 8388608 | tf_op jit(solution)/shard_map/jit(_roll_dynamic)/dynamic_slice | solution.py:47
  112.6 3.9 %constant_dynamic-slice_fusion = (bf16[16,1,256,256]{3,2,1,0:T(8,128)(2,1)S(1)}, bf16[16,256,256]{2,1,0:T(8,128)(2,1)}) fusion(bf16[16,2,256,256]{3,2,1,0:T(8,128)(2,1)} %bitcast.34, s32[]{:T(128)S(6)} %select_n.43, s32[]{:T(128)S(6)} %select_n.44), kind=kLoop, calls=%fused_computation.34 | loop fusion | bytes 8388616 | tf_op jit(solution)/shard_map/jit(dynamic_index_in_dim)/dynamic_slice | solution.py:53
  116.6 6.5 %collective-permute-start.7 = (bf16[16,256,256]{2,1,0:T(8,128)(2,1)}, bf16[16,256,256]{2,1,0:T(8,128)(2,1)}, u32[]{:S(2)}, u32[]{:S(2)}) collective-permute-start(bf16[16,256,256]{2,1,0:T(8,128)(2,1)} %get-tuple-element.13), channel_id=1, source_target_pairs={{0,1},{1,0},{2,3},{3,2},{4,5},{5,4},{6,7},{7,6},{8,9},{9,8},{10,11... | collective-permute-start | bytes 6291464 | tf_op jit(solution)/shard_map/ppermute | solution.py:17
  123.3 3.9 %collective-permute-done.7 = bf16[16,256,256]{2,1,0:T(8,128)(2,1)} collective-permute-done((bf16[16,256,256]{2,1,0:T(8,128)(2,1)}, bf16[16,256,256]{2,1,0:T(8,128)(2,1)}, u32[]{:S(2)}, u32[]{:S(2)}) %collective-permute-start.7) | collective-permute-done | bytes 2097184 | tf_op jit(solution)/shard_map/ppermute | solution.py:17
  127.2 3.9 %bitcast_select_fusion.1 = (bf16[4096,256]{1,0:T(8,128)(2,1)}, bf16[4096,256]{1,0:T(8,128)(2,1)}) fusion(bf16[16,256,256]{2,1,0:T(8,128)(2,1)} %collective-permute-done.7, bf16[16,1,256,256]{3,2,1,0:T(8,128)(2,1)S(1)} %get-tuple-element.12, pred[]{:T(512)S(6)} %eq.38), kind=kLoop, calls=%fused_computation.5 | loop fusion | flops 2097152 | bytes 8388609 | tf_op jit(solution)/shard_map/jit(_where)/select_n | solution.py:58
  131.2 8.3 %fusion = f32[1024,512]{0,1:T(8,128)S(1)} fusion(bf16[1024,4096]{0,1:T(8,128)(2,1)} %all-gather.2.cloned.1.call-done, bf16[4096,256]{1,0:T(8,128)(2,1)} %get-tuple-element.11, bf16[4096,256]{1,0:T(8,128)(2,1)} %get-tuple-element.10), kind=kOutput, calls=%fused_computation | convolution fusion | flops 4303355904 | bytes 14680064 | tf_op jit(solution)/shard_map/dot_general | solution.py:61
  139.5 5.4 %all_to_all.5 = f32[2,1024,256]{1,2,0:T(8,128)S(1)} all-to-all(f32[2,1024,256]{1,2,0:T(8,128)S(1)} %bitcast.35), channel_id=1, replica_groups=mesh['row'=8,'col_0'=4,'col_1'=4,'layer'=2] {'layer'}, dimensions={0} | all-to-all | bytes 4194304 | tf_op jit(solution)/shard_map/all_to_all | solution.py:28
  144.9 1.2 reduce_sum.18
  146.1 2.3 %select_reduce_fusion = (f32[]{:T(128)}, f32[1024,256]{0,1:T(8,128)S(1)}) fusion(s32[1024]{0:T(1024)S(1)} %iota_add_fusion, s32[256]{0:T(256)S(1)} %iota_add_fusion.1, f32[1024,2]{0,1:T(2,128)S(1)} %bitcast.36, f32[1024,256]{0,1:T(8,128)} %reduce_sum.18, bf16[1024,256]{0,1:T(8,128)(2,1)S(1)} %copy-done, pred[1024]{0:T(1024)(128)(4,1)S(1)} %broadcast_bitcast_fusion.2), kind=kLoop, calls=%fused_computation.9 | loop fusion | flops 2097151 | bytes 2635780 | tf_op jit(solution)/shard_map/reduce_sum | solution.py:77
  148.4 11.4 %psum.28 = f32[]{:T(128)} all-reduce(f32[]{:T(128)} %get-tuple-element.8), channel_id=1, replica_groups=mesh['row'=8,'col_0'=4,'col_1'=4,'layer'=2] {'row'}, use_global_device_ids=true, to_apply=%region_2.3 | all-reduce | flops 1 | bytes 8 | tf_op jit(solution)/shard_map/psum | solution.py:33
  159.8 9.3 %psum.29 = f32[]{:T(128)} all-reduce(f32[]{:T(128)} %psum.28), channel_id=1, replica_groups=mesh['row'=8,'col_0'=4,'col_1'=4,'layer'=2] {'col_0'}, use_global_device_ids=true, to_apply=%region_3.4 | all-reduce | flops 1 | bytes 8 | tf_op jit(solution)/shard_map/psum | solution.py:33
  169.1 8.9 %psum.30 = f32[]{:T(128)} all-reduce(f32[]{:T(128)} %psum.29), channel_id=1, replica_groups=mesh['row'=8,'col_0'=4,'col_1'=4,'layer'=2] {'col_1'}, use_global_device_ids=true, to_apply=%region_4.5 | all-reduce | flops 1 | bytes 8 | tf_op jit(solution)/shard_map/psum | solution.py:33
  178.0 1.3 copy.14
  179.3 10.5 %psum.31 = f32[]{:T(128)} all-reduce(f32[]{:T(128)} %psum.30), channel_id=1, replica_groups=mesh['row'=8,'col_0'=4,'col_1'=4,'layer'=2] {'layer'}, use_global_device_ids=true, to_apply=%region_5.6 | all-reduce | flops 1 | bytes 8 | tf_op jit(solution)/shard_map/psum | solution.py:33
  (42 shorter events, 7.6 us)
Async XLA Ops:
  7.2 124.0 %all-gather.2.cloned.1.call-start = ((), (), s32[]{:S(2)}) async-start(), calls=%async_computation.1 | async-start | bytes 8912896 | tf_op jit(solution)/shard_map/all_gather | solution.py:62
  10.1 93.9 %copy-start = (bf16[1024,256]{0,1:T(8,128)(2,1)S(1)}, bf16[1024,256]{0,1:T(8,128)(2,1)}, u32[]{:S(2)}) copy-start(bf16[1024,256]{0,1:T(8,128)(2,1)} %bitcast_multiply_fusion) | copy-start | bytes 1572868
  10.1 18.3 %collective-permute-start = (bf16[1024,256]{0,1:T(8,128)(2,1)}, bf16[1024,256]{0,1:T(8,128)(2,1)S(1)}, u32[]{:S(2)}, u32[]{:S(2)}) collective-permute-start(bf16[1024,256]{0,1:T(8,128)(2,1)} %bitcast_multiply_fusion), channel_id=1, source_target_pairs={{0,32},{32,64},{64,96},{96,128},{128,160},{160,192},{192,224},{224... | collective-permute-start | bytes 1572872 | tf_op jit(solution)/shard_map/ppermute | solution.py:46
  28.4 13.5 %collective-permute-start.1 = (bf16[1024,256]{0,1:T(8,128)(2,1)S(1)}, bf16[1024,256]{0,1:T(8,128)(2,1)S(1)}, u32[]{:S(2)}, u32[]{:S(2)}) collective-permute-start(bf16[1024,256]{0,1:T(8,128)(2,1)S(1)} %collective-permute-done), channel_id=1, source_target_pairs={{0,32},{32,64},{64,96},{96,128},{128,160},{160,192},{192,224},{224... | collective-permute-start | bytes 1572872 | tf_op jit(solution)/shard_map/ppermute | solution.py:46
  41.9 12.6 %collective-permute-start.2 = (bf16[1024,256]{0,1:T(8,128)(2,1)S(1)}, bf16[1024,256]{0,1:T(8,128)(2,1)S(1)}, u32[]{:S(2)}, u32[]{:S(2)}) collective-permute-start(bf16[1024,256]{0,1:T(8,128)(2,1)S(1)} %collective-permute-done.1), channel_id=1, source_target_pairs={{0,32},{32,64},{64,96},{96,128},{128,160},{160,192},{192,224},{224... | collective-permute-start | bytes 1572872 | tf_op jit(solution)/shard_map/ppermute | solution.py:46
  54.5 11.8 %collective-permute-start.3 = (bf16[1024,256]{0,1:T(8,128)(2,1)S(1)}, bf16[1024,256]{0,1:T(8,128)(2,1)S(1)}, u32[]{:S(2)}, u32[]{:S(2)}) collective-permute-start(bf16[1024,256]{0,1:T(8,128)(2,1)S(1)} %collective-permute-done.2), channel_id=1, source_target_pairs={{0,32},{32,64},{64,96},{96,128},{128,160},{160,192},{192,224},{224... | collective-permute-start | bytes 1572872 | tf_op jit(solution)/shard_map/ppermute | solution.py:46
  66.3 10.9 %collective-permute-start.4 = (bf16[1024,256]{0,1:T(8,128)(2,1)S(1)}, bf16[1024,256]{0,1:T(8,128)(2,1)S(1)}, u32[]{:S(2)}, u32[]{:S(2)}) collective-permute-start(bf16[1024,256]{0,1:T(8,128)(2,1)S(1)} %collective-permute-done.3), channel_id=1, source_target_pairs={{0,32},{32,64},{64,96},{96,128},{128,160},{160,192},{192,224},{224... | collective-permute-start | bytes 1572872 | tf_op jit(solution)/shard_map/ppermute | solution.py:46
  77.2 10.5 %collective-permute-start.5 = (bf16[1024,256]{0,1:T(8,128)(2,1)S(1)}, bf16[1024,256]{0,1:T(8,128)(2,1)}, u32[]{:S(2)}, u32[]{:S(2)}) collective-permute-start(bf16[1024,256]{0,1:T(8,128)(2,1)S(1)} %collective-permute-done.4), channel_id=1, source_target_pairs={{0,32},{32,64},{64,96},{96,128},{128,160},{160,192},{192,224},{224... | collective-permute-start | bytes 1572872 | tf_op jit(solution)/shard_map/ppermute | solution.py:46
  87.7 10.4 %collective-permute-start.6 = (bf16[1024,256]{0,1:T(8,128)(2,1)}, bf16[1024,256]{0,1:T(8,128)(2,1)}, u32[]{:S(2)}, u32[]{:S(2)}) collective-permute-start(bf16[1024,256]{0,1:T(8,128)(2,1)} %collective-permute-done.5), channel_id=1, source_target_pairs={{0,32},{32,64},{64,96},{96,128},{128,160},{160,192},{192,224},{224... | collective-permute-start | bytes 1572872 | tf_op jit(solution)/shard_map/ppermute | solution.py:46
  106.2 16.9 %copy-start.1 = (s32[8,2]{0,1:T(2,128)S(1)}, s32[8,2]{0,1:T(2,128)}, u32[]{:S(2)}) copy-start(s32[8,2]{0,1:T(2,128)} %param.6) | copy-start | bytes 196
  106.2 17.0 %copy-start.2 = (s32[8]{0:T(128)S(1)}, s32[8]{0:T(128)}, u32[]{:S(2)}) copy-start(s32[8]{0:T(128)} %param.7) | copy-start | bytes 100
  116.6 10.7 %collective-permute-start.7 = (bf16[16,256,256]{2,1,0:T(8,128)(2,1)}, bf16[16,256,256]{2,1,0:T(8,128)(2,1)}, u32[]{:S(2)}, u32[]{:S(2)}) collective-permute-start(bf16[16,256,256]{2,1,0:T(8,128)(2,1)} %get-tuple-element.13), channel_id=1, source_target_pairs={{0,1},{1,0},{2,3},{3,2},{4,5},{5,4},{6,7},{7,6},{8,9},{9,8},{10,11... | collective-permute-start | bytes 6291464 | tf_op jit(solution)/shard_map/ppermute | solution.py:17
Sparse Core Ops, SparseCore 0:
  11.0 79.5 all-gather.1
